TPU v7x, 256 devices: a whole 4x4x8 slice. The times are simulated.
256 devices in a mesh: section: 16 (over x, y_hi, core), ulysses: 8 (over z), batch: 2 (over y_lo).
Axes of the slice: x: 4, y: 4 (y_hi: 2, y_lo: 2; y = y_hi * 2 + y_lo), z: 8, core: 2. Of those that a mesh axis runs over, the one named last changes fastest.
Arguments:
- incoming: float32 [32, 512, 3072], P(('batch', 'section'), 'ulysses'), parts along dimension 0, may hold values from -6 to 6
- plan: int32 [16], P('section'), may hold values from 0 to 7
- stale_kv: bfloat16 [32, 4096, 24, 256], P(('batch', 'section'), None, 'ulysses'), parts along dimension 0, may hold values from -60 to 60
- qkv_weight: bfloat16 [16, 3072, 24, 384], P('section', None, 'ulysses'), may hold values from -0.109375 to 0.109375
- out_weight: bfloat16 [16, 24, 128, 3072], P('section', 'ulysses'), may hold values from -0.109375 to 0.109375
- q_gain: float32 [16, 128], P('section'), may hold values from 0.7 to 6
- k_gain: float32 [16, 128], P('section'), may hold values from 0.5 to 1.5
- shift_mod: float32 [16, 3072], P('section'), may hold values from -4 to 4
- scale_mod: float32 [16, 3072], P('section'), may hold values from -2.5 to 2.5
- gate_mod: float32 [16, 3072], P('section'), may hold values from -4 to 4
Outputs:
- block_out: float32 [32, 512, 3072], P(('batch', 'section'), 'ulysses'), parts along dimension 0
- fresh_kv: bfloat16 [32, 512, 24, 256], P(('batch', 'section'), None, 'ulysses'), parts along dimension 0
There are 2 independent parts, one for each index of `batch`. A program takes and returns all parts, laid end to end along the dimension named above; an argument that names none is the same for every part. Nothing has to cross between parts.
All inputs are finite; a program needn't handle non-finite values.
Results may differ from a plain program's by a relative error of at most 0.015.
The roundings to bfloat16 on the way count: a program that leaves them out, or rounds other values in their place, can miss the bound.
Values may be sent and summed in bfloat16 or wider, within the bound.
No kernel may reach another device: no remote copies, remote signals or barrier semaphores. Data moves between devices by JAX's collectives and lax.ppermute only.
A program may use at most 192 MiB of HBM per device.

v0:
```python
import math

import jax
import jax.numpy as jnp
from jax import lax
from jax.sharding import PartitionSpec as P


def from_behind(block, axis, distance):
    devices = range(lax.axis_size(axis))
    route = [((i - distance) % len(devices), i) for i in devices]
    return lax.ppermute(block, axis, route)


def normalize(rows, shift_row, scale_row):
    mean = jnp.mean(rows, -1, keepdims=True)
    centered = rows - mean
    var = jnp.mean(centered * centered, -1, keepdims=True)
    return (centered * lax.rsqrt(var + 1e-06) * (1.0 + scale_row) + shift_row).astype(jnp.bfloat16)


def head_norm(values, gain):
    return values * lax.rsqrt(jnp.mean(values * values, -1, keepdims=True) + 1e-06) * gain


def on_device(
    incoming, plan, stale_kv, qkv_weight, out_weight, q_gain, k_gain, shift_mod, scale_mod, gate_mod
):
    rows = incoming.shape[1]
    local_heads = stale_kv.shape[2]
    head_size = stale_kv.shape[3] // 2
    rank = lax.axis_index("ulysses")
    weight_cols = qkv_weight[0].reshape(qkv_weight.shape[1], local_heads * 3 * head_size)
    sent = lax.all_gather(incoming[0], "ulysses", axis=0, tiled=True)
    patch = from_behind(sent, "section", 1)
    own = lax.dynamic_slice_in_dim(patch, rank * rows, rows, 0)
    qkv = jnp.dot(
        normalize(patch, shift_mod[0], scale_mod[0]),
        weight_cols,
        preferred_element_type=jnp.float32,
    )
    total_rows = qkv.shape[0]
    qkv = qkv.reshape(total_rows, local_heads, 3 * head_size)
    query = head_norm(qkv[:, :, :head_size], q_gain[0]).astype(jnp.bfloat16)
    keyed = head_norm(qkv[:, :, head_size : 2 * head_size], k_gain[0]).astype(jnp.bfloat16)
    valued = qkv[:, :, 2 * head_size :].astype(jnp.bfloat16)
    fresh = jnp.concatenate([keyed, valued], -1)
    start = plan[0] * total_rows
    zero = jnp.zeros((), jnp.int32)
    keys = lax.dynamic_update_slice(stale_kv[0], fresh, (start, zero, zero))
    scores = jnp.einsum(
        "qhd,khd->hqk", query, keys[:, :, :head_size], preferred_element_type=jnp.float32
    ) / math.sqrt(head_size)
    weights = jax.nn.softmax(scores, -1).astype(jnp.bfloat16)
    attn = jnp.einsum(
        "hqk,khd->qhd", weights, keys[:, :, head_size:], preferred_element_type=jnp.float32
    ).astype(jnp.bfloat16)
    attn = attn.reshape(total_rows, local_heads * head_size)
    w_rows = out_weight[0].reshape(local_heads * head_size, out_weight.shape[3])
    term = jnp.dot(attn, w_rows, preferred_element_type=jnp.float32).astype(jnp.bfloat16)
    proj = lax.psum_scatter(
        lax.optimization_barrier(term).astype(jnp.float32).astype(jnp.bfloat16),
        "ulysses",
        scatter_dimension=0,
        tiled=True,
    ).astype(jnp.float32)
    block_out = own + gate_mod[0] * proj
    return (block_out[None], fresh[None])


def solution(mesh):
    return jax.shard_map(
        on_device,
        mesh=mesh,
        in_specs=(
            P(("batch", "section"), "ulysses", None),
            P("section"),
            P(("batch", "section"), None, "ulysses", None),
            P("section", None, "ulysses", None),
            P("section", "ulysses", None, None),
            P("section", None),
            P("section", None),
            P("section", None),
            P("section", None),
            P("section", None),
        ),
        out_specs=(
            P(("batch", "section"), "ulysses", None),
            P(("batch", "section"), None, "ulysses", None),
        ),
        check_vma=False,
    )
```

profile of v0, /device:TPU:2, one launch (start us, length us, event | category | flops | bytes accessed | tf_op | source)
XLA Modules:
  0.0 296.2 jit_solution(13832431943626216396)
XLA Ops:
  7.2 0.0 all-gather.3.cloned.1.call-start
  7.2 5.9 %copy.26 = bf16[1,4096,3,256]{3,1,2,0:T(8,128)(2,1)} copy(bf16[1,4096,3,256]{3,1,2,0:T(8,128)(2,1)} %param.12) | data formatting | bytes 12582912
  13.2 0.0 all-gather.3.cloned.1.call-update
  13.2 0.0 reduce-scatter.2.cloned.1.call-start
  13.2 77.5 %all-gather.3.cloned.1.call-done = f32[1,512,3072]{2,1,0:T(8,128)} async-done(((f32[1,64,3072]{2,1,0:T(8,128)}), f32[1,512,3072]{2,1,0:T(8,128)}) %all-gather.3.cloned.1.call-update) | async-done | bytes 6291472 | tf_op jit(solution)/shard_map/all_gather | solution.py:34
  90.8 10.3 %copy.16 = bf16[1,3072,3,384]{1,3,2,0:T(8,128)(2,1)} copy(bf16[1,3072,3,384]{3,1,2,0:T(8,128)(2,1)} %param.13) | data formatting | bytes 14155776 | tf_op args[3]
  101.8 62.1 %collective-permute-done = f32[512,3072]{1,0:T(8,128)} collective-permute-done((f32[512,3072]{1,0:T(8,128)}, f32[512,3072]{1,0:T(8,128)}, u32[]{:S(2)}, u32[]{:S(2)}) %collective-permute-start) | collective-permute-done | bytes 6291488 | tf_op jit(solution)/shard_map/ppermute | solution.py:12
  163.9 3.1 %reduce_sum.45 = f32[512]{0:T(512)S(1)} reduce(f32[512,3072]{1,0:T(8,128)} %collective-permute-done, f32[]{:T(128)} %constant.12.clone.1), dimensions={1}, to_apply=%region_0.0 | reduce | flops 1572352 | bytes 6293508 | tf_op jit(solution)/shard_map/reduce_sum | solution.py:16
  167.1 3.5 %multiply_reduce_fusion.1 = f32[512]{0:T(512)S(1)} fusion(f32[512,3072]{1,0:T(8,128)} %collective-permute-done, f32[512]{0:T(512)S(1)} %broadcast_multiply_fusion), kind=kLoop, calls=%fused_computation.10 | loop fusion | flops 4718080 | bytes 6295552 | tf_op jit(solution)/shard_map/reduce_sum | solution.py:18
  170.6 8.3 %fusion.6 = f32[512,3,384]{0,2,1:T(8,128)S(1)} fusion(bf16[1,3072,3,384]{1,3,2,0:T(8,128)(2,1)} %copy.16, f32[512,3072]{1,0:T(8,128)} %collective-permute-done, f32[3072]{0:T(1024)S(1)} %bitcast.35, f32[3072]{0:T(1024)S(1)} %bitcast.31, f32[512]{0:T(512)S(1)} %add_rsqrt_fusion.2, f32[512]{0:T(512)S(1)} %broadcast_multiply_fusion), kind=kOutput, calls=%fused_computation.7 | convolution fusion | flops 3631742976 | bytes 15757312 | tf_op jit(solution)/shard_map/dot_general | solution.py:37
  179.0 0.2 multiply_reduce_fusion.2
  179.2 0.1 slice.38
  179.3 1.2 copy-done.1
  180.4 0.1 multiply_convert_fusion.1
  180.5 1.3 fusion.23
  181.8 1.4 copy.17
  183.2 0.9 constant_dynamic-update-slice_fusion
  184.2 14.0 %fusion.10 = f32[3,512,4096]{2,1,0:T(8,128)} fusion(bf16[4096,3,256]{2,0,1:T(8,128)(2,1)} %constant_dynamic-update-slice_fusion, f32[512,3,384]{0,2,1:T(8,128)} %copy-done.1, f32[128]{0:T(128)S(1)} %bitcast.32, f32[512,3]{0,1:T(4,128)S(1)} %get-tuple-element.12), kind=kOutput, calls=%fused_computation.13 | convolution fusion | flops 1611202560 | bytes 29104640 | tf_op jit(solution)/shard_map/qhd,khd->hqk/dot_general | solution.py:51
  198.1 29.2 %fusion.24 = (f32[3,512]{1,0:T(4,128)S(1)}, f32[3,512,4096]{2,1,0:T(8,128)}) fusion(f32[3,512,4096]{2,1,0:T(8,128)} %fusion.10), kind=kOutput, calls=%fused_computation.38 | output fusion | flops 25169920 | bytes 50337792 | tf_op jit(solution)/shard_map/sub | solution.py:54
  227.4 11.4 %fusion.17 = bf16[3,128,512]{2,1,0:T(8,128)(2,1)S(1)} fusion(f32[3,512,4096]{2,1,0:T(8,128)} %get-tuple-element.11, f32[3,512]{1,0:T(4,128)S(1)} %get-tuple-element.10, bf16[4096,3,256]{2,0,1:T(8,128)(2,1)} %constant_dynamic-update-slice_fusion), kind=kOutput, calls=%fused_computation.20 | convolution fusion | flops 1623392256 | bytes 28710912 | tf_op jit(solution)/shard_map/hqk,khd->qhd/dot_general | solution.py:55
  238.9 3.5 %convolution_convert_fusion = bf16[512,3072]{1,0:T(8,128)(2,1)} fusion(bf16[512,384]{0,1:T(8,128)(2,1)S(1)} %bitcast.36, bf16[384,3072]{1,0:T(8,128)(2,1)S(1)} %bitcast.28), kind=kOutput, calls=%fused_computation.11 | convolution fusion | flops 1209532416 | bytes 5898240 | tf_op jit(solution)/shard_map/dot_general | solution.py:60
  242.4 1.2 copy.20
  243.6 43.5 %reduce-scatter.2.cloned.1.call-done = bf16[64,3072]{1,0:T(8,128)(2,1)} async-done(((bf16[512,3072]{1,0:T(8,128)(2,1)}), bf16[64,3072]{1,0:T(8,128)(2,1)}) %reduce-scatter.2.cloned.1.call-update) | async-done | bytes 393232 | tf_op jit(solution)/shard_map/reduce_scatter | solution.py:61
  287.1 2.2 add_bitcast_fusion
  (21 shorter events, 0.1 us)
Async XLA Ops:
  7.2 231.7 %copy-start = (bf16[1,3,128,3072]{3,2,1,0:T(8,128)(2,1)S(1)}, bf16[1,3,128,3072]{3,2,1,0:T(8,128)(2,1)}, u32[]{:S(2)}) copy-start(bf16[1,3,128,3072]{3,2,1,0:T(8,128)(2,1)} %param.14) | copy-start | bytes 7077892
  7.2 83.6 %all-gather.3.cloned.1.call-start = ((), (), s32[]{:S(2)}) async-start(), calls=%async_computation.2 | async-start | bytes 7077888 | tf_op jit(solution)/shard_map/all_gather | solution.py:34
  13.2 273.9 %reduce-scatter.2.cloned.1.call-start = ((), (), s32[]{:S(2)}) async-start(), calls=%async_computation.1 | async-start | bytes 3538944 | tf_op jit(solution)/shard_map/reduce_scatter | solution.py:61
  90.8 10.9 %copy-start.4 = (f32[1,3072]{1,0:T(1,128)S(1)}, f32[1,3072]{1,0:T(1,128)}, u32[]{:S(2)}) copy-start(f32[1,3072]{1,0:T(1,128)} %param.18) | copy-start | bytes 36868
  90.8 73.1 %collective-permute-start = (f32[512,3072]{1,0:T(8,128)}, f32[512,3072]{1,0:T(8,128)}, u32[]{:S(2)}, u32[]{:S(2)}) collective-permute-start(f32[512,3072]{1,0:T(8,128)} %bitcast.34), channel_id=1, source_target_pairs={{240,0},{0,16},{16,32},{32,48},{48,64},{64,80},{80,96},{96,112},{1... | collective-permute-start | bytes 18874376 | tf_op jit(solution)/shard_map/ppermute | solution.py:12
  101.7 68.9 %copy-start.7 = (f32[1,3072]{1,0:T(1,128)S(1)}, f32[1,3072]{1,0:T(1,128)}, u32[]{:S(2)}) copy-start(f32[1,3072]{1,0:T(1,128)} %param.17) | copy-start | bytes 36868
  170.6 9.8 %copy-start.6 = (f32[1,128]{1,0:T(1,128)S(1)}, f32[1,128]{1,0:T(1,128)}, u32[]{:S(2)}) copy-start(f32[1,128]{1,0:T(1,128)} %param.16) | copy-start | bytes 1540
  178.9 1.5 copy-start.1
  179.0 5.2 %copy-start.5 = (f32[1,128]{1,0:T(1,128)S(1)}, f32[1,128]{1,0:T(1,128)}, u32[]{:S(2)}) copy-start(f32[1,128]{1,0:T(1,128)} %param.15) | copy-start | bytes 1540
  238.8 3.6 %copy-start.2 = (bf16[1,512,3,256]{1,3,2,0:T(8,128)(2,1)S(1)}, bf16[1,512,3,256]{1,3,2,0:T(8,128)(2,1)}, u32[]{:S(2)}) copy-start(bf16[1,512,3,256]{1,3,2,0:T(8,128)(2,1)} %get-tuple-element.8) | copy-start | bytes 2359300
  238.8 48.3 %copy-start.3 = (f32[1,3072]{1,0:T(1,128)S(1)}, f32[1,3072]{1,0:T(1,128)}, u32[]{:S(2)}) copy-start(f32[1,3072]{1,0:T(1,128)} %param.19) | copy-start | bytes 36868
Sparse Core Ops, SparseCore 0:
  13.3 77.4 all-gather.2
  242.5 44.5 reduce-scatter.1
where the time goes:
time: 297 us; the launch traced here: 296 us
  waiting for transfers between devices  183 us (62%)
  other arithmetic  39.8 us (13%)
  matrix products  37.2 us (13%)
  local copies, waits for them, and re-layouts  21 us (7%)
  between operations  14.8 us (5%)
    all_gather x1, waiting for transfers between devices, on_device(): sent = lax.all_gather(incoming[0], 'ulysses', axis=0, tiled=True)  77.5 us
    ppermute x1, waiting for transfers between devices, from_behind(): return lax.ppermute(block, axis, route)  62.1 us
    reduce_scatter x1, waiting for transfers between devices, on_device(): lax.psum_scatter(lax.optimization_barrier(term).astype(jnp.float32).astyp...  43.5 us
    sub x1, other arithmetic, on_device(): weights = jax.nn.softmax(scores, -1).astype(jnp.bfloat16)  29.2 us
    unnamed x19, local copies, waits for them, and re-layouts  18.6 us
    dot_general x1, matrix products, on_device(): jnp.einsum('qhd,khd->hqk', query, keys[:, :, :head_size], preferred_eleme...  14 us
    dot_general x1, matrix products, on_device(): jnp.einsum('hqk,khd->qhd', weights, keys[:, :, head_size:], preferred_ele...  11.4 us
    dot_general x1, matrix products, on_device(): jnp.dot(normalize(patch, shift_mod[0], scale_mod[0]), weight_cols, prefer...  8.31 us
  transfers between devices with their start and end apart: 3, of which 3 were waited for; matrix products, arithmetic and copies ran while one was open for 4% of the time, Pallas kernels for 0%

commit v1 on v0

v1 whole, which is shorter than its diff:
```python
import functools
import math

import jax
import jax.numpy as jnp
from jax import lax
from jax.experimental import pallas as pl
from jax.experimental.pallas import tpu as pltpu
from jax.sharding import PartitionSpec as P

LANES = 128
NT = (((1,), (1,)), ((), ()))
MIB = 2**20


def score_scale(head_size):
    return math.log2(math.e) / math.sqrt(head_size)


def norm_kernel(x_ref, shift_ref, scale_ref, out_ref):
    rows = x_ref[...]
    centered = rows - jnp.mean(rows, -1, keepdims=True)
    var = jnp.mean(centered * centered, -1, keepdims=True)
    out_ref[...] = (
        centered * lax.rsqrt(var + 1e-06) * (1.0 + scale_ref[...]) + shift_ref[...]
    ).astype(jnp.bfloat16)


def normalize(rows, shift_row, scale_row):
    return pl.pallas_call(
        norm_kernel,
        out_shape=jax.ShapeDtypeStruct(rows.shape, jnp.bfloat16),
        cost_estimate=pl.CostEstimate(flops=8 * rows.size, bytes_accessed=6 * rows.size, transcendentals=0),
    )(rows, shift_row, scale_row)


def head_norm(values, gain):
    return (values * lax.rsqrt(jnp.mean(values * values, -1, keepdims=True) + 1e-06) * gain).astype(
        jnp.bfloat16
    )


def stale_kernel(n_rows, patch, plan_ref, *refs):
    row_refs = refs[:n_rows]
    w_ref, kv_ref, q_gain_ref, k_gain_ref, q_out, fresh_out, top_out, den_out, num_out = refs[n_rows:]
    head = kv_ref.shape[2] // 2
    scale = score_scale(head)
    rows = [r[...] for r in row_refs]
    rows = jnp.concatenate(rows, 0) if n_rows > 1 else rows[0]
    qkv = jnp.dot(rows, w_ref[0], preferred_element_type=jnp.float32)
    query = head_norm(qkv[:, :head], q_gain_ref[...])
    q_out[0] = query
    fresh_out[0, :, :head] = head_norm(qkv[:, head : 2 * head], k_gain_ref[...])
    fresh_out[0, :, head:] = qkv[:, 2 * head :].astype(jnp.bfloat16)
    plan = plan_ref[0]
    ones = jnp.ones((patch, head), jnp.bfloat16)
    top = None
    for j in range(kv_ref.shape[1] // patch - 1):
        block = j + (j >= plan).astype(jnp.int32)
        at = pl.ds(pl.multiple_of(block * patch, patch), patch)
        scores = lax.dot_general(query, kv_ref[0, at, :head], NT, preferred_element_type=jnp.float32)
        new_top = jnp.max(scores, -1, keepdims=True) * scale
        if top is not None:
            new_top = jnp.maximum(top, new_top)
        weights = jnp.exp2(scores * scale - new_top).astype(jnp.bfloat16)
        values = jnp.concatenate([kv_ref[0, at, head:], ones], 1)
        term = jnp.dot(weights, values, preferred_element_type=jnp.float32)
        total = term if top is None else total * jnp.exp2(top - new_top) + term
        top = new_top
    top_out[0] = jnp.broadcast_to(top, top_out.shape[1:])
    num_out[0] = total[:, :head]
    den_out[0] = total[:, head:]


def stale_part(plan, rows, weight, kv, q_gain, k_gain):
    heads, width, cols = weight.shape
    seq, pair = kv.shape[1:]
    head = pair // 2
    count = sum(r.shape[0] for r in rows)
    patch = 512

    def whole(a):
        return pl.BlockSpec(a.shape, lambda h, p: (0,) * a.ndim)

    def by_head(*shape):
        return pl.BlockSpec((1,) + shape, lambda h, p: (h, 0, 0))

    flat = jax.ShapeDtypeStruct((heads, count, head), jnp.float32)
    return pl.pallas_call(
        functools.partial(stale_kernel, len(rows), patch),
        grid_spec=pltpu.PrefetchScalarGridSpec(
            num_scalar_prefetch=1,
            grid=(heads,),
            in_specs=[whole(r) for r in rows]
            + [by_head(width, cols), by_head(seq, pair), whole(q_gain), whole(k_gain)],
            out_specs=[by_head(count, head), by_head(count, pair)] + [by_head(count, head)] * 3,
        ),
        out_shape=[
            jax.ShapeDtypeStruct((heads, count, head), jnp.bfloat16),
            jax.ShapeDtypeStruct((heads, count, pair), jnp.bfloat16),
            flat,
            flat,
            flat,
        ],
        compiler_params=pltpu.CompilerParams(vmem_limit_bytes=40 * MIB),
        cost_estimate=pl.CostEstimate(
            flops=2 * count * heads * (width * cols + seq * pair),
            bytes_accessed=13 * MIB,
            transcendentals=count * heads * seq,
        ),
    )(plan, *rows, weight, kv, q_gain, k_gain)


def fresh_kernel(q_ref, top_ref, den_ref, num_ref, fresh_ref, w_ref, term_ref):
    heads, count = q_ref.shape[0], fresh_ref.shape[1]
    head = q_ref.shape[2]
    scale = score_scale(head)
    ones = jnp.ones((count, head), jnp.bfloat16)
    parts = []
    for h in range(heads):
        scores = lax.dot_general(q_ref[h], fresh_ref[h, :, :head], NT, preferred_element_type=jnp.float32)
        top = top_ref[h]
        new_top = jnp.maximum(top, jnp.max(scores, -1, keepdims=True) * scale)
        weights = jnp.exp2(scores * scale - jnp.concatenate([new_top] * (count // head), 1))
        values = jnp.concatenate([fresh_ref[h, :, head:], ones], 1)
        term = jnp.dot(weights.astype(jnp.bfloat16), values, preferred_element_type=jnp.float32)
        shrink = jnp.exp2(top - new_top)
        num = num_ref[h] * shrink + term[:, :head]
        den = den_ref[h] * shrink + term[:, head:]
        parts.append((num / den).astype(jnp.bfloat16))
    attn = jnp.concatenate(parts, 1)
    term_ref[...] = jnp.dot(attn, w_ref[...], preferred_element_type=jnp.float32).astype(jnp.bfloat16)


def fresh_part(query, top, den, num, fresh, weight):
    heads, count, head = query.shape
    return pl.pallas_call(
        fresh_kernel,
        out_shape=jax.ShapeDtypeStruct((count, weight.shape[1]), jnp.bfloat16),
        compiler_params=pltpu.CompilerParams(vmem_limit_bytes=40 * MIB),
        cost_estimate=pl.CostEstimate(
            flops=2 * count * (weight.size + 2 * heads * fresh.shape[1] * head),
            bytes_accessed=4 * MIB,
            transcendentals=count * heads * fresh.shape[1],
        ),
    )(query, top, den, num, fresh, weight)


def on_device(
    incoming, plan, stale_kv, qkv_weight, out_weight, q_gain, k_gain, shift_mod, scale_mod, gate_mod
):
    kv = jnp.transpose(stale_kv[0], (1, 0, 2))
    weight = jnp.transpose(qkv_weight[0], (1, 0, 2))
    w_rows = out_weight[0].reshape(-1, out_weight.shape[3])
    blocks = lax.axis_size("section")
    own = lax.ppermute(incoming[0], "section", [((i - 1) % blocks, i) for i in range(blocks)])
    modulated = normalize(own, shift_mod, scale_mod)
    rows = lax.all_gather(modulated, "ulysses", axis=0, tiled=True)
    query, fresh, top, den, num = stale_part(plan, [rows], weight, kv, q_gain, k_gain)
    term = fresh_part(query, top, den, num, fresh, w_rows)
    proj = lax.psum_scatter(term, "ulysses", scatter_dimension=0, tiled=True).astype(jnp.float32)
    block_out = own + gate_mod[0] * proj
    return (block_out[None], jnp.transpose(fresh, (1, 0, 2))[None])


def solution(mesh):
    return jax.shard_map(
        on_device,
        mesh=mesh,
        in_specs=(
            P(("batch", "section"), "ulysses", None),
            P("section"),
            P(("batch", "section"), None, "ulysses", None),
            P("section", None, "ulysses", None),
            P("section", "ulysses", None, None),
            P("section", None),
            P("section", None),
            P("section", None),
            P("section", None),
            P("section", None),
        ),
        out_specs=(
            P(("batch", "section"), "ulysses", None),
            P(("batch", "section"), None, "ulysses", None),
        ),
        check_vma=False,
    )
```

time: 297 us -> 154 us (0.52)
  waiting for transfers between devices: 183 us -> 106 us
  other arithmetic: 39.8 us -> 1.95 us
  matrix products: 37.2 us -> 0 us
  Pallas kernels: 0 us -> 22.6 us
  local copies, waits for them, and re-layouts: 21 us -> 8.01 us
    ppermute x1, waiting for transfers between devices: 62.1 us -> 14 us  [on_device(): lax.ppermute(incoming[0], 'section', [((i - 1) % blocks, i) for i in rang...]
    dot_general x4 -> x0, matrix products: 37.2 us -> none  [the longest x1 14 us: on_device(): jnp.einsum('qhd,khd->hqk', query, keys[:, :, :head_size], preferred_eleme...]
    all_gather x1, waiting for transfers between devices: 77.5 us -> 46.5 us  [on_device(): rows = lax.all_gather(modulated, 'ulysses', axis=0, tiled=True)]
    sub x1 -> x0, other arithmetic: 29.2 us -> none  [on_device(): weights = jax.nn.softmax(scores, -1).astype(jnp.bfloat16)]
    pallas_call x0 -> x3, Pallas kernels: none -> 22.6 us  [the longest x1 15.6 us: stale_part(): pl.pallas_call(functools.partial(stale_kernel, len(rows), patch), grid_sp...]
    unnamed x19 -> x18, local copies, waits for them, and re-layouts: 18.6 us -> 8.01 us
    reduce_sum x3 -> x0, other arithmetic: 6.89 us -> none  [the longest x1 3.54 us: normalize(): var = jnp.mean(centered * centered, -1, keepdims=True)]
  transfers between devices with their start and end apart: 3 -> 3, of which waited for: 3 -> 3; matrix products, arithmetic and copies ran while one was open for 4% -> 0% of each run, Pallas kernels for 0% -> 0%
where the time goes in v1:
time: 154 us
  waiting for transfers between devices  106 us (69%)
  Pallas kernels  22.6 us (15%)
  between operations  14.7 us (10%)
  local copies, waits for them, and re-layouts  8.01 us (5%)
  other arithmetic  1.95 us (1%)
    all_gather x1, waiting for transfers between devices, on_device(): rows = lax.all_gather(modulated, 'ulysses', axis=0, tiled=True)  46.5 us
    reduce_scatter x1, waiting for transfers between devices, on_device(): lax.psum_scatter(term, 'ulysses', scatter_dimension=0, tiled=True)  45.6 us
    pallas_call x1, Pallas kernels, stale_part(): pl.pallas_call(functools.partial(stale_kernel, len(rows), patch), grid_sp...  15.6 us
    ppermute x1, waiting for transfers between devices, on_device(): lax.ppermute(incoming[0], 'section', [((i - 1) % blocks, i) for i in rang...  14 us
    unnamed x18, local copies, waits for them, and re-layouts  8.01 us
    pallas_call x1, Pallas kernels, fresh_part(): pl.pallas_call(fresh_kernel, out_shape=jax.ShapeDtypeStruct((count, weigh...  4.84 us
  transfers between devices with their start and end apart: 3, of which 3 were waited for; matrix products, arithmetic and copies ran while one was open for 0% of the time, Pallas kernels for 0%

profile of v1, /device:TPU:2, one launch (start us, length us, event | category | flops | bytes accessed | tf_op | source)
XLA Modules:
  0.0 153.6 jit_solution(901386501622269802)
XLA Ops:
  7.2 0.0 all-gather.2.cloned.1.call-start
  7.2 0.1 collective-permute-start
  7.3 14.0 %collective-permute-done.x_ref = f32[64,3072]{1,0:T(8,128)S(1)} collective-permute-done((f32[64,3072]{1,0:T(8,128)}, f32[64,3072]{1,0:T(8,128)S(1)}, u32[]{:S(2)}, u32[]{:S(2)}) %collective-permute-start) | collective-permute-done | bytes 786464 | tf_op jit(solution)/shard_map/ppermute | solution.py:156
  21.3 0.0 copy-start.6
  21.3 0.9 copy-done.6
  22.2 2.2 %shard_map.113 = bf16[64,3072]{1,0:T(8,128)(2,1)} custom-call(f32[64,3072]{1,0:T(8,128)} %copy-done.6, f32[1,3072]{1,0:T(1,128)} %shift_ref.1, f32[1,3072]{1,0:T(1,128)} %scale_ref.1), custom_call_target="tpu_custom_call" | custom-call | flops 1572864 | bytes 1179648 | tf_op jit(solution)/shard_map/pallas_call | solution.py:30
  24.4 0.0 all-gather.2.cloned.1.call-update
  24.4 0.0 reduce-scatter.2.cloned.1.call-start
  25.1 46.5 %all-gather.2.cloned.1.call-done.refs_0_ = bf16[512,3072]{1,0:T(8,128)(2,1)} async-done(((bf16[64,3072]{1,0:T(8,128)(2,1)}), bf16[512,3072]{1,0:T(8,128)(2,1)}) %all-gather.2.cloned.1.call-update) | async-done | bytes 3145744 | tf_op jit(solution)/shard_map/all_gather | solution.py:158
  71.6 0.0 copy-start.2
  71.6 2.8 %copy-done.2 = bf16[1,4096,3,256]{3,1,2,0:T(8,128)(2,1)S(1)} copy-done((bf16[1,4096,3,256]{3,1,2,0:T(8,128)(2,1)S(1)}, bf16[1,4096,3,256]{3,1,2,0:T(8,128)(2,1)}, u32[]{:S(2)}) %copy-start.2) | copy-done | bytes 6291480
  74.4 0.0 copy-start.3
  74.4 1.9 %copy-done.3 = bf16[512,3072]{1,0:T(8,128)(2,1)S(1)} copy-done((bf16[512,3072]{1,0:T(8,128)(2,1)S(1)}, bf16[512,3072]{1,0:T(8,128)(2,1)}, u32[]{:S(2)}) %copy-start.3) | copy-done | bytes 3145752
  76.3 0.7 copy-done.4
  77.0 0.7 copy-done.5
  77.6 15.6 %shard_map.114 = (bf16[3,512,128]{2,1,0:T(8,128)(2,1)S(1)}, bf16[3,512,256]{2,1,0:T(8,128)(2,1)}, f32[3,512,128]{2,1,0:T(8,128)S(1)}, f32[3,512,128]{2,1,0:T(8,128)S(1)}, f32[3,512,128]{2,1,0:T(8,128)S(1)}) custom-call(s32[1]{0:T(128)S(6)} %copy.12.plan_ref, bf16[512,3072]{1,0:T(8,128)(2,1)S(1)} %copy-done.3, bf16[3,3072,384]{2,1,0:T(8,128)(2,1)} %bitcast.18, ...), custom_call_target="tpu_custom_call" | custom-call | flops 6845104128 | bytes 13631488 | tf_op jit(solution)/shard_map/pallas_call | solution.py:89
  93.2 0.0 copy-done
  93.2 1.1 copy-done.1
  94.3 4.8 %shard_map.115 = bf16[512,3072]{1,0:T(8,128)(2,1)} custom-call(bf16[3,512,128]{2,1,0:T(8,128)(2,1)S(1)} %get-tuple-element.7.q_ref, f32[3,512,128]{2,1,0:T(8,128)S(1)} %get-tuple-element.8.top_ref, f32[3,512,128]{2,1,0:T(8,128)S(1)} %get-tuple-element.9.den_ref, f32[3,512,128]{2,1,0:T(8,128)S(1)} %get-tuple-element.10.num_ref, ...), custom_call_target="tpu_custom_call" | custom-call | flops 1610612736 | bytes 4194304 | tf_op jit(solution)/shard_map/pallas_call | solution.py:137
  99.2 0.0 reduce-scatter.2.cloned.1.call-update
  99.2 45.6 %reduce-scatter.2.cloned.1.call-done = bf16[64,3072]{1,0:T(8,128)(2,1)} async-done(((bf16[512,3072]{1,0:T(8,128)(2,1)}), bf16[64,3072]{1,0:T(8,128)(2,1)}) %reduce-scatter.2.cloned.1.call-update) | async-done | bytes 393232 | tf_op jit(solution)/shard_map/reduce_scatter | solution.py:161
  144.8 0.0 copy-done.7
  144.8 0.0 copy-done.8
  144.8 2.0 %add_bitcast_fusion = f32[1,64,3072]{2,1,0:T(8,128)} fusion(f32[64,3072]{1,0:T(8,128)S(1)} %copy-done.7, bf16[64,3072]{1,0:T(8,128)(2,1)} %reduce-scatter.2.cloned.1.call-done, f32[3072]{0:T(1024)S(1)} %bitcast.17), kind=kLoop, calls=%fused_computation | loop fusion | flops 589824 | bytes 1978368 | tf_op jit(solution)/shard_map/broadcast_in_dim | solution.py:163
  (6 shorter events, 0.0 us)
Async XLA Ops:
  7.2 64.5 %all-gather.2.cloned.1.call-start = ((), (), s32[]{:S(2)}) async-start(), calls=%async_computation.1 | async-start | bytes 3538944 | tf_op jit(solution)/shard_map/all_gather | solution.py:158
  7.2 14.1 %collective-permute-start = (f32[64,3072]{1,0:T(8,128)}, f32[64,3072]{1,0:T(8,128)S(1)}, u32[]{:S(2)}, u32[]{:S(2)}) collective-permute-start(f32[64,3072]{1,0:T(8,128)} %bitcast.19), channel_id=1, source_target_pairs={{240,0},{0,16},{16,32},{32,48},{48,64},{64,80},{80,96},{96,112},{1... | collective-permute-start | bytes 2359304 | tf_op jit(solution)/shard_map/ppermute | solution.py:156
  21.3 0.9 copy-start.6
  24.4 120.3 %reduce-scatter.2.cloned.1.call-start = ((), (), s32[]{:S(2)}) async-start(), calls=%async_computation.2 | async-start | bytes 3538944 | tf_op jit(solution)/shard_map/reduce_scatter | solution.py:161
  71.6 2.8 %copy-start.2 = (bf16[1,4096,3,256]{3,1,2,0:T(8,128)(2,1)S(1)}, bf16[1,4096,3,256]{3,1,2,0:T(8,128)(2,1)}, u32[]{:S(2)}) copy-start(bf16[1,4096,3,256]{3,1,2,0:T(8,128)(2,1)} %param.12) | copy-start | bytes 18874372
  74.4 1.9 %copy-start.3 = (bf16[512,3072]{1,0:T(8,128)(2,1)S(1)}, bf16[512,3072]{1,0:T(8,128)(2,1)}, u32[]{:S(2)}) copy-start(bf16[512,3072]{1,0:T(8,128)(2,1)} %all-gather.2.cloned.1.call-done.refs_0_) | copy-start | bytes 9437188
  76.3 0.7 copy-start.4
  77.0 0.7 copy-start.5
  77.6 15.6 %copy-start = (bf16[1,3,128,3072]{3,2,1,0:T(8,128)(2,1)S(1)}, bf16[1,3,128,3072]{3,2,1,0:T(8,128)(2,1)}, u32[]{:S(2)}) copy-start(bf16[1,3,128,3072]{3,2,1,0:T(8,128)(2,1)} %param.14) | copy-start | bytes 7077892
  93.2 1.1 copy-start.1
  99.2 45.6 %copy-start.7 = (f32[64,3072]{1,0:T(8,128)S(1)}, f32[64,3072]{1,0:T(8,128)}, u32[]{:S(2)}) copy-start(f32[64,3072]{1,0:T(8,128)} %copy-done.6) | copy-start | bytes 2359300
  99.2 45.6 %copy-start.8 = (f32[1,3072]{1,0:T(1,128)S(1)}, f32[1,3072]{1,0:T(1,128)}, u32[]{:S(2)}) copy-start(f32[1,3072]{1,0:T(1,128)} %param.19) | copy-start | bytes 36868
Sparse Core Ops, SparseCore 0:
  24.6 47.0 all-gather.1
  99.3 45.3 reduce-scatter.1

commit v2 on v1

v2 whole, which is shorter than its diff:
```python
import functools
import math

import jax
import jax.numpy as jnp
from jax import lax
from jax.experimental import pallas as pl
from jax.experimental.pallas import tpu as pltpu
from jax.sharding import PartitionSpec as P

NT = (((1,), (1,)), ((), ()))
MIB = 2**20


def score_scale(head_size):
    return math.log2(math.e) / math.sqrt(head_size)


def norm_kernel(x_ref, shift_ref, scale_ref, first_ref, second_ref):
    rows = x_ref[...]
    centered = rows - jnp.mean(rows, -1, keepdims=True)
    var = jnp.mean(centered * centered, -1, keepdims=True)
    modulated = (
        centered * lax.rsqrt(var + 1e-06) * (1.0 + scale_ref[...]) + shift_ref[...]
    ).astype(jnp.bfloat16)
    half = first_ref.shape[0]
    first_ref[...] = modulated[:half]
    second_ref[...] = modulated[half:]


def normalize(rows, shift_row, scale_row):
    return pl.pallas_call(
        norm_kernel,
        out_shape=[jax.ShapeDtypeStruct((rows.shape[0] // 2, rows.shape[1]), jnp.bfloat16)] * 2,
        cost_estimate=pl.CostEstimate(flops=8 * rows.size, bytes_accessed=6 * rows.size, transcendentals=0),
    )(rows, shift_row, scale_row)


def head_norm(values, gain):
    return (values * lax.rsqrt(jnp.mean(values * values, -1, keepdims=True) + 1e-06) * gain).astype(
        jnp.bfloat16
    )


def project_rows(row_refs, w_ref, q_gain_ref, k_gain_ref, q_out, fresh_out):
    head = q_out.shape[2]
    rows = [r[...] for r in row_refs]
    rows = jnp.concatenate(rows, 0) if len(rows) > 1 else rows[0]
    qkv = jnp.dot(rows, w_ref[0], preferred_element_type=jnp.float32)
    query = head_norm(qkv[:, :head], q_gain_ref[...])
    q_out[0] = query
    fresh_out[0, :, :head] = head_norm(qkv[:, head : 2 * head], k_gain_ref[...])
    fresh_out[0, :, head:] = qkv[:, 2 * head :].astype(jnp.bfloat16)
    return query


def attend_stale(patch, plan, query, kv_ref, top_out, den_out, num_out):
    head = query.shape[1]
    scale = score_scale(head)
    ones = jnp.ones((patch, head), jnp.bfloat16)
    top = None
    for j in range(kv_ref.shape[1] // patch - 1):
        block = j + (j >= plan).astype(jnp.int32)
        at = pl.ds(pl.multiple_of(block * patch, patch), patch)
        scores = lax.dot_general(query, kv_ref[0, at, :head], NT, preferred_element_type=jnp.float32)
        new_top = jnp.max(scores, -1, keepdims=True) * scale
        if top is not None:
            new_top = jnp.maximum(top, new_top)
        weights = jnp.exp2(scores * scale - new_top).astype(jnp.bfloat16)
        values = jnp.concatenate([kv_ref[0, at, head:], ones], 1)
        term = jnp.dot(weights, values, preferred_element_type=jnp.float32)
        total = term if top is None else total * jnp.exp2(top - new_top) + term
        top = new_top
    top_out[0] = jnp.broadcast_to(top, top_out.shape[1:])
    num_out[0] = total[:, :head]
    den_out[0] = total[:, head:]


def whole(a):
    return pl.BlockSpec(a.shape, lambda h, *p: (0,) * a.ndim)


def by_head(*shape):
    return pl.BlockSpec((1,) + shape, lambda h, *p: (h, 0, 0))


def both_kernel(n_rows, patch, plan_ref, *refs):
    w_ref, kv_ref, q_gain_ref, k_gain_ref, q_out, fresh_out, top_out, den_out, num_out = refs[n_rows:]
    query = project_rows(refs[:n_rows], w_ref, q_gain_ref, k_gain_ref, q_out, fresh_out)
    attend_stale(patch, plan_ref[0], query, kv_ref, top_out, den_out, num_out)


def project_and_attend(patch, plan, rows, weight, kv, q_gain, k_gain):
    heads, width, cols = weight.shape
    seq, pair = kv.shape[1:]
    head = pair // 2
    count = sum(r.shape[0] for r in rows)
    flat = jax.ShapeDtypeStruct((heads, count, head), jnp.float32)
    return pl.pallas_call(
        functools.partial(both_kernel, len(rows), patch),
        grid_spec=pltpu.PrefetchScalarGridSpec(
            num_scalar_prefetch=1,
            grid=(heads,),
            in_specs=[whole(r) for r in rows]
            + [by_head(width, cols), by_head(seq, pair), whole(q_gain), whole(k_gain)],
            out_specs=[by_head(count, head), by_head(count, pair)] + [by_head(count, head)] * 3,
        ),
        out_shape=[
            jax.ShapeDtypeStruct((heads, count, head), jnp.bfloat16),
            jax.ShapeDtypeStruct((heads, count, pair), jnp.bfloat16),
            flat,
            flat,
            flat,
        ],
        compiler_params=pltpu.CompilerParams(vmem_limit_bytes=24 * MIB),
        cost_estimate=pl.CostEstimate(
            flops=2 * count * heads * (width * cols + seq * pair),
            bytes_accessed=13 * MIB,
            transcendentals=count * heads * seq,
        ),
    )(plan, *rows, weight, kv, q_gain, k_gain)


def project_kernel(n_rows, *refs):
    w_ref, q_gain_ref, k_gain_ref, q_out, fresh_out = refs[n_rows:]
    project_rows(refs[:n_rows], w_ref, q_gain_ref, k_gain_ref, q_out, fresh_out)


def project(rows, weight, q_gain, k_gain):
    heads, width, cols = weight.shape
    head = cols // 3
    count = sum(r.shape[0] for r in rows)
    return pl.pallas_call(
        functools.partial(project_kernel, len(rows)),
        grid=(heads,),
        in_specs=[whole(r) for r in rows] + [by_head(width, cols), whole(q_gain), whole(k_gain)],
        out_specs=[by_head(count, head), by_head(count, 2 * head)],
        out_shape=[
            jax.ShapeDtypeStruct((heads, count, head), jnp.bfloat16),
            jax.ShapeDtypeStruct((heads, count, 2 * head), jnp.bfloat16),
        ],
        compiler_params=pltpu.CompilerParams(vmem_limit_bytes=16 * MIB),
        cost_estimate=pl.CostEstimate(
            flops=2 * count * weight.size, bytes_accessed=7 * MIB, transcendentals=0
        ),
    )(*rows, weight, q_gain, k_gain)


def stale_kernel(patch, plan_ref, q_ref, kv_ref, top_out, den_out, num_out):
    attend_stale(patch, plan_ref[0], q_ref[0], kv_ref, top_out, den_out, num_out)


def attend(patch, plan, query, kv):
    heads, count, head = query.shape
    seq = kv.shape[1]
    return pl.pallas_call(
        functools.partial(stale_kernel, patch),
        grid_spec=pltpu.PrefetchScalarGridSpec(
            num_scalar_prefetch=1,
            grid=(heads,),
            in_specs=[by_head(count, head), by_head(seq, 2 * head)],
            out_specs=[by_head(count, head)] * 3,
        ),
        out_shape=[jax.ShapeDtypeStruct((heads, count, head), jnp.float32)] * 3,
        compiler_params=pltpu.CompilerParams(vmem_limit_bytes=16 * MIB),
        cost_estimate=pl.CostEstimate(
            flops=4 * query.size * seq, bytes_accessed=6 * MIB, transcendentals=count * heads * seq
        ),
    )(plan, query, kv)


def fresh_kernel(n_fresh, q_ref, top_ref, den_ref, num_ref, w_ref, *refs):
    fresh_refs, term_refs = refs[:n_fresh], refs[n_fresh:]
    heads, _, head = q_ref.shape
    count = sum(r.shape[1] for r in fresh_refs)
    scale = score_scale(head)
    ones = jnp.ones((count, head), jnp.bfloat16)
    parts = []
    for h in range(heads):
        fresh = jnp.concatenate([r[h] for r in fresh_refs], 0)
        scores = lax.dot_general(q_ref[h], fresh[:, :head], NT, preferred_element_type=jnp.float32)
        top = top_ref[h]
        new_top = jnp.maximum(top, jnp.max(scores, -1, keepdims=True) * scale)
        weights = jnp.exp2(scores * scale - jnp.concatenate([new_top] * (count // head), 1))
        values = jnp.concatenate([fresh[:, head:], ones], 1)
        term = jnp.dot(weights.astype(jnp.bfloat16), values, preferred_element_type=jnp.float32)
        shrink = jnp.exp2(top - new_top)
        num = num_ref[h] * shrink + term[:, :head]
        den = den_ref[h] * shrink + term[:, head:]
        parts.append((num / den).astype(jnp.bfloat16))
    attn = jnp.concatenate(parts, 1)
    terms = jnp.dot(attn, w_ref[...], preferred_element_type=jnp.float32).astype(jnp.bfloat16)
    size = term_refs[0].shape[0]
    for i, r in enumerate(term_refs):
        r[...] = terms[i * size : (i + 1) * size]


def fresh_terms(state, fresh, weight, pieces):
    query = state[0]
    heads, count, head = query.shape
    total = sum(f.shape[1] for f in fresh)
    return pl.pallas_call(
        functools.partial(fresh_kernel, len(fresh)),
        out_shape=[jax.ShapeDtypeStruct((count // pieces, weight.shape[1]), jnp.bfloat16)] * pieces,
        compiler_params=pltpu.CompilerParams(vmem_limit_bytes=16 * MIB),
        cost_estimate=pl.CostEstimate(
            flops=2 * count * (weight.size + 2 * heads * total * head),
            bytes_accessed=4 * MIB,
            transcendentals=count * heads * total,
        ),
    )(*state, weight, *fresh)


def join(partial, term):
    return (partial.astype(jnp.float32) + term.astype(jnp.float32)).astype(jnp.bfloat16)


def on_device(
    incoming, plan, stale_kv, qkv_weight, out_weight, q_gain, k_gain, shift_mod, scale_mod, gate_mod
):
    kv = jnp.transpose(stale_kv[0], (1, 0, 2))
    weight = jnp.transpose(qkv_weight[0], (1, 0, 2))
    w_rows = out_weight[0].reshape(-1, out_weight.shape[3])
    blocks, ring = lax.axis_size("section"), lax.axis_size("ulysses")
    rank = lax.axis_index("ulysses")
    shard = incoming.shape[1]
    half, patch = shard // 2, shard * ring
    far = ring // 2

    def up(chunk):
        return lax.ppermute(chunk, "ulysses", [(i, (i + 1) % ring) for i in range(ring)])

    def down(chunk):
        return lax.ppermute(chunk, "ulysses", [((i + 1) % ring, i) for i in range(ring)])

    own = lax.ppermute(incoming[0], "section", [((i - 1) % blocks, i) for i in range(blocks)])
    first, second = normalize(own, shift_mod, scale_mod)

    below, above = {0: (first, second)}, {0: (first, second)}
    for d in range(1, far):
        below[d] = (up(below[d - 1][0]), up(below[d - 1][1]))
        b = down(above[d - 1][1])
        above[d] = (down(above[d - 1][0]), b)
    last = (up(below[far - 1][0]), down(above[far - 1][1]))

    groups = [project_and_attend(patch, plan, [first, second], weight, kv, q_gain, k_gain)]
    for d in range(1, far):
        groups.append(
            project_and_attend(patch, plan, [*below[d], *above[d]], weight, kv, q_gain, k_gain)
        )
    last_query, last_fresh = project(last, weight, q_gain, k_gain)
    fresh = [g[1] for g in groups] + [last_fresh]

    def terms(state, pieces):
        return fresh_terms((state[0], *state[2:]), fresh, w_rows, pieces)

    low_a, low_b, high_a, high_b = terms(groups[far - 1], 4)
    up_b, down_a = up(high_b), down(low_a)
    last_state = (last_query, last_fresh, *attend(patch, plan, last_query, kv))
    far_a, far_b = terms(last_state, 2)
    up_a, down_b = up(far_a), down(far_b)
    for d in range(far - 1, 0, -1):
        up_a, down_b = up(join(up_a, high_a)), down(join(down_b, low_b))
        if d > 1:
            low_a, low_b, high_a, high_b = terms(groups[d - 1], 4)
            up_b, down_a = up(join(up_b, high_b)), down(join(down_a, low_a))
    own_a, own_b = terms(groups[0], 2)

    def total(a, b, c):
        return a.astype(jnp.float32) + b.astype(jnp.float32) + c.astype(jnp.float32)

    proj = jnp.concatenate([total(own_a, up_a, down_a), total(own_b, up_b, down_b)], 0)
    block_out = own + gate_mod[0] * proj

    shards = [f[:, :shard] for f in fresh[far - 1 : 0 : -1]] + [fresh[0]]
    shards += [f[:, shard:] for f in fresh[1:far]] + [last_fresh]
    twice = jnp.concatenate(shards + shards, 1)
    start = (far - 1 - rank) % ring * shard
    ordered = lax.dynamic_slice_in_dim(twice, start, patch, 1)
    return (block_out[None], jnp.transpose(ordered, (1, 0, 2))[None])


def solution(mesh):
    return jax.shard_map(
        on_device,
        mesh=mesh,
        in_specs=(
            P(("batch", "section"), "ulysses", None),
            P("section"),
            P(("batch", "section"), None, "ulysses", None),
            P("section", None, "ulysses", None),
            P("section", "ulysses", None, None),
            P("section", None),
            P("section", None),
            P("section", None),
            P("section", None),
            P("section", None),
        ),
        out_specs=(
            P(("batch", "section"), "ulysses", None),
            P(("batch", "section"), None, "ulysses", None),
        ),
        check_vma=False,
    )
```

time: 154 us -> 131 us (0.85); the launches traced: 154 us -> 128 us
  waiting for transfers between devices: 106 us -> 37.4 us
  starting transfers between devices: 0.16 us -> 45.1 us
  between operations: 14.7 us -> 1.83 us
  Pallas kernels: 22.6 us -> 31.5 us
  local copies, waits for them, and re-layouts: 8.01 us -> 11 us
    all_gather x1 -> x0, waiting for transfers between devices: 46.5 us -> none  [on_device(): rows = lax.all_gather(modulated, 'ulysses', axis=0, tiled=True)]
    reduce_scatter x1 -> x0, waiting for transfers between devices: 45.6 us -> none  [on_device(): lax.psum_scatter(term, 'ulysses', scatter_dimension=0, tiled=True)]
    ppermute x0 -> x28, starting transfers between devices: none -> 45.1 us  [the longest x14 38 us: down(): lax.ppermute(chunk, 'ulysses', [((i + 1) % ring, i) for i in range(ring)])]
    ppermute x0 -> x28, waiting for transfers between devices: none -> 23.4 us  [the longest x14 22.1 us: up(): lax.ppermute(chunk, 'ulysses', [(i, (i + 1) % ring) for i in range(ring)])]
    pallas_call x3 -> x12, Pallas kernels: 22.6 us -> 31.5 us  [the longest x4 19.1 us: project_and_attend(): pl.pallas_call(functools.partial(both_kernel, len(rows), patch), grid_spe...]
    unnamed x18 -> x45, local copies, waits for them, and re-layouts: 8.01 us -> 10 us
  transfers between devices with their start and end apart: 3 -> 29, of which waited for: 3 -> 8; matrix products, arithmetic and copies ran while one was open for 0% -> 1% of each run, Pallas kernels for 0% -> 15%
where the time goes in v2:
time: 131 us; the launch traced here: 128 us
  starting transfers between devices  45.1 us (34%)
  waiting for transfers between devices  37.4 us (29%)
  Pallas kernels  31.5 us (24%)
  local copies, waits for them, and re-layouts  11 us (8%)
  between operations  1.83 us (1%)
  other arithmetic  1.59 us (1%)
    ppermute x14, starting transfers between devices, down(): lax.ppermute(chunk, 'ulysses', [((i + 1) % ring, i) for i in range(ring)])  38 us
    ppermute x14, waiting for transfers between devices, up(): lax.ppermute(chunk, 'ulysses', [(i, (i + 1) % ring) for i in range(ring)])  22.1 us
    pallas_call x4, Pallas kernels, project_and_attend(): pl.pallas_call(functools.partial(both_kernel, len(rows), patch), grid_spe...  19.1 us
    ppermute x1, waiting for transfers between devices, on_device(): lax.ppermute(incoming[0], 'section', [((i - 1) % blocks, i) for i in rang...  14 us
    unnamed x45, local copies, waits for them, and re-layouts  10 us
    ppermute x14, starting transfers between devices, up(): lax.ppermute(chunk, 'ulysses', [(i, (i + 1) % ring) for i in range(ring)])  7.02 us
    pallas_call x5, Pallas kernels, fresh_terms(): pl.pallas_call(functools.partial(fresh_kernel, len(fresh)), out_shape=[ja...  5.43 us
    pallas_call x1, Pallas kernels, attend(): pl.pallas_call(functools.partial(stale_kernel, patch), grid_spec=pltpu.Pr...  2.96 us
  transfers between devices with their start and end apart: 29, of which 8 were waited for; matrix products, arithmetic and copies ran while one was open for 1% of the time, Pallas kernels for 15%

profile of v2, /device:TPU:2, one launch (start us, length us, event | category | flops | bytes accessed | tf_op | source)
XLA Modules:
  0.0 128.4 jit_solution(9438358651529570693)
XLA Ops:
  0.7 14.0 %collective-permute-done.x_ref = f32[64,3072]{1,0:T(8,128)S(1)} collective-permute-done((f32[64,3072]{1,0:T(8,128)}, f32[64,3072]{1,0:T(8,128)S(1)}, u32[]{:S(2)}, u32[]{:S(2)}) %collective-permute-start) | collective-permute-done | bytes 786464 | tf_op jit(solution)/shard_map/ppermute | solution.py:236
  15.6 2.2 %shard_map.113 = (bf16[32,3072]{1,0:T(8,128)(2,1)}, bf16[32,3072]{1,0:T(8,128)(2,1)}) custom-call(f32[64,3072]{1,0:T(8,128)} %copy-done.10, f32[1,3072]{1,0:T(1,128)} %shift_ref.1, f32[1,3072]{1,0:T(1,128)} %scale_ref.1), custom_call_target="tpu_custom_call" | custom-call | flops 1572864 | bytes 1179648 | tf_op jit(solution)/shard_map/pallas_call | solution.py:32
  21.7 2.1 %collective-permute-start.3 = (bf16[32,3072]{1,0:T(8,128)(2,1)}, bf16[32,3072]{1,0:T(8,128)(2,1)S(1)}, u32[]{:S(2)}, u32[]{:S(2)}) collective-permute-start(bf16[32,3072]{1,0:T(8,128)(2,1)} %get-tuple-element.45.refs_0_), channel_id=1, source_target_pairs={{2,0},{4,2},{6,4},{8,6},{10,8},{12,10},{14,12},{0,14},{3,1},{5,3},... | collective-permute-start | bytes 589832 | tf_op jit(solution)/shard_map/ppermute | solution.py:234
  25.7 4.0 %collective-permute-done.1.refs_0_ = bf16[32,3072]{1,0:T(8,128)(2,1)S(1)} collective-permute-done((bf16[32,3072]{1,0:T(8,128)(2,1)}, bf16[32,3072]{1,0:T(8,128)(2,1)S(1)}, u32[]{:S(2)}, u32[]{:S(2)}) %collective-permute-start.1) | collective-permute-done | bytes 196640 | tf_op jit(solution)/shard_map/ppermute | solution.py:231
  29.7 4.2 %collective-permute-done.2.refs_1_ = bf16[32,3072]{1,0:T(8,128)(2,1)S(1)} collective-permute-done((bf16[32,3072]{1,0:T(8,128)(2,1)}, bf16[32,3072]{1,0:T(8,128)(2,1)S(1)}, u32[]{:S(2)}, u32[]{:S(2)}) %collective-permute-start.2) | collective-permute-done | bytes 196640 | tf_op jit(solution)/shard_map/ppermute | solution.py:231
  33.9 3.2 %collective-permute-start.7 = (bf16[32,3072]{1,0:T(8,128)(2,1)S(1)}, bf16[32,3072]{1,0:T(8,128)(2,1)S(1)}, u32[]{:S(2)}, u32[]{:S(2)}) collective-permute-start(bf16[32,3072]{1,0:T(8,128)(2,1)S(1)} %collective-permute-done.3.refs_2_), channel_id=1, source_target_pairs={{2,0},{4,2},{6,4},{8,6},{10,8},{12,10},{14,12},{0,14},{3,1},{5,3},... | collective-permute-start | bytes 589832 | tf_op jit(solution)/shard_map/ppermute | solution.py:234
  38.6 3.0 %copy-done = bf16[1,3072,3,384]{3,1,2,0:T(8,128)(2,1)S(1)} copy-done((bf16[1,3072,3,384]{3,1,2,0:T(8,128)(2,1)S(1)}, bf16[1,3072,3,384]{3,1,2,0:T(8,128)(2,1)}, u32[]{:S(2)}) %copy-start) | copy-done | bytes 7077912
  41.6 2.8 %copy-done.2 = bf16[1,4096,3,256]{3,1,2,0:T(8,128)(2,1)S(1)} copy-done((bf16[1,4096,3,256]{3,1,2,0:T(8,128)(2,1)S(1)}, bf16[1,4096,3,256]{3,1,2,0:T(8,128)(2,1)}, u32[]{:S(2)}) %copy-start.2) | copy-done | bytes 6291480
  47.6 5.4 %shard_map.114 = (bf16[3,64,128]{2,1,0:T(8,128)(2,1)S(1)}, bf16[3,64,256]{2,1,0:T(8,128)(2,1)S(1)}, f32[3,64,128]{2,1,0:T(8,128)S(1)}, f32[3,64,128]{2,1,0:T(8,128)S(1)}, f32[3,64,128]{2,1,0:T(8,128)S(1)}) custom-call(s32[1]{0:T(128)S(6)} %copy.27.plan_ref, bf16[32,3072]{1,0:T(8,128)(2,1)S(1)} %copy-done.4, bf16[32,3072]{1,0:T(8,128)(2,1)S(1)} %copy-done.5, ...), custom_call_target="tpu_custom_call" | custom-call | flops 855638016 | bytes 13631488 | tf_op jit(solution)/shard_map/pallas_call | solution.py:99
  54.4 3.1 %collective-permute-start.11 = (bf16[32,3072]{1,0:T(8,128)(2,1)S(1)}, bf16[32,3072]{1,0:T(8,128)(2,1)S(1)}, u32[]{:S(2)}, u32[]{:S(2)}) collective-permute-start(bf16[32,3072]{1,0:T(8,128)(2,1)S(1)} %collective-permute-done.7.refs_2_), channel_id=1, source_target_pairs={{2,0},{4,2},{6,4},{8,6},{10,8},{12,10},{14,12},{0,14},{3,1},{5,3},... | collective-permute-start | bytes 589832 | tf_op jit(solution)/shard_map/ppermute | solution.py:234
  58.4 4.4 %shard_map.115 = (bf16[3,128,128]{2,1,0:T(8,128)(2,1)S(1)}, bf16[3,128,256]{2,1,0:T(8,128)(2,1)S(1)}, f32[3,128,128]{2,1,0:T(8,128)S(1)}, f32[3,128,128]{2,1,0:T(8,128)S(1)}, f32[3,128,128]{2,1,0:T(8,128)S(1)}) custom-call(s32[1]{0:T(128)S(6)} %copy.27.plan_ref, bf16[32,3072]{1,0:T(8,128)(2,1)S(1)} %collective-permute-done.1.refs_0_, ...), custom_call_target="tpu_custom_call" | custom-call | flops 1711276032 | bytes 13631488 | tf_op jit(solution)/shard_map/pallas_call | solution.py:99
  62.9 4.6 %shard_map.116 = (bf16[3,128,128]{2,1,0:T(8,128)(2,1)S(1)}, bf16[3,128,256]{2,1,0:T(8,128)(2,1)S(1)}, f32[3,128,128]{2,1,0:T(8,128)S(1)}, f32[3,128,128]{2,1,0:T(8,128)S(1)}, f32[3,128,128]{2,1,0:T(8,128)S(1)}) custom-call(s32[1]{0:T(128)S(6)} %copy.27.plan_ref, bf16[32,3072]{1,0:T(8,128)(2,1)S(1)} %collective-permute-done.5.refs_0_, ...), custom_call_target="tpu_custom_call" | custom-call | flops 1711276032 | bytes 13631488 | tf_op jit(solution)/shard_map/pallas_call | solution.py:99
  67.6 4.6 %shard_map.117 = (bf16[3,128,128]{2,1,0:T(8,128)(2,1)S(1)}, bf16[3,128,256]{2,1,0:T(8,128)(2,1)S(1)}, f32[3,128,128]{2,1,0:T(8,128)S(1)}, f32[3,128,128]{2,1,0:T(8,128)S(1)}, f32[3,128,128]{2,1,0:T(8,128)S(1)}) custom-call(s32[1]{0:T(128)S(6)} %copy.27.plan_ref, bf16[32,3072]{1,0:T(8,128)(2,1)S(1)} %collective-permute-done.9.refs_0_, ...), custom_call_target="tpu_custom_call" | custom-call | flops 1711276032 | bytes 13631488 | tf_op jit(solution)/shard_map/pallas_call | solution.py:99
  75.6 3.6 %collective-permute-done.13.refs_0_ = bf16[32,3072]{1,0:T(8,128)(2,1)S(1)} collective-permute-done((bf16[32,3072]{1,0:T(8,128)(2,1)S(1)}, bf16[32,3072]{1,0:T(8,128)(2,1)S(1)}, u32[]{:S(2)}, u32[]{:S(2)}) %collective-permute-start.13) | collective-permute-done | bytes 196640 | tf_op jit(solution)/shard_map/ppermute | solution.py:231
  81.1 3.0 %shard_map.120 = (f32[3,64,128]{2,1,0:T(8,128)S(1)}, f32[3,64,128]{2,1,0:T(8,128)S(1)}, f32[3,64,128]{2,1,0:T(8,128)S(1)}) custom-call(s32[1]{0:T(128)S(6)} %copy.27.plan_ref, bf16[3,64,128]{2,1,0:T(8,128)(2,1)S(1)} %get-tuple-element.57.q_ref, bf16[3,4096,256]{2,1,0:T(8,128)(2,1)S(1)} %bitcast.26), custom_call_target="tpu_custom_call" | custom-call | flops 402653184 | bytes 6291456 | tf_op jit(solution)/shard_map/pallas_call | solution.py:156
  85.1 3.3 %collective-permute-start.25 = (bf16[32,3072]{1,0:T(8,128)(2,1)S(1)}, bf16[32,3072]{1,0:T(8,128)(2,1)S(1)}, u32[]{:S(2)}, u32[]{:S(2)}) collective-permute-start(bf16[32,3072]{1,0:T(8,128)(2,1)S(1)} %get-tuple-element.84), channel_id=1, source_target_pairs={{2,0},{4,2},{6,4},{8,6},{10,8},{12,10},{14,12},{0,14},{3,1},{5,3},... | collective-permute-start | bytes 589832 | tf_op jit(solution)/shard_map/ppermute | solution.py:234
  89.7 3.2 %collective-permute-start.19 = (bf16[32,3072]{1,0:T(8,128)(2,1)S(1)}, bf16[32,3072]{1,0:T(8,128)(2,1)S(1)}, u32[]{:S(2)}, u32[]{:S(2)}) collective-permute-start(bf16[32,3072]{1,0:T(8,128)(2,1)S(1)} %get-tuple-element.77), channel_id=1, source_target_pairs={{2,0},{4,2},{6,4},{8,6},{10,8},{12,10},{14,12},{0,14},{3,1},{5,3},... | collective-permute-start | bytes 589832 | tf_op jit(solution)/shard_map/ppermute | solution.py:234
  97.3 3.3 %collective-permute-start.26 = (bf16[32,3072]{1,0:T(8,128)(2,1)S(1)}, bf16[32,3072]{1,0:T(8,128)(2,1)S(1)}, u32[]{:S(2)}, u32[]{:S(2)}) collective-permute-start(bf16[32,3072]{1,0:T(8,128)(2,1)S(1)} %add_convert_fusion.2), channel_id=1, source_target_pairs={{2,0},{4,2},{6,4},{8,6},{10,8},{12,10},{14,12},{0,14},{3,1},{5,3},... | collective-permute-start | bytes 589832 | tf_op jit(solution)/shard_map/ppermute | solution.py:234
  100.8 3.3 %collective-permute-start.20 = (bf16[32,3072]{1,0:T(8,128)(2,1)S(1)}, bf16[32,3072]{1,0:T(8,128)(2,1)S(1)}, u32[]{:S(2)}, u32[]{:S(2)}) collective-permute-start(bf16[32,3072]{1,0:T(8,128)(2,1)S(1)} %add_convert_fusion.6), channel_id=1, source_target_pairs={{2,0},{4,2},{6,4},{8,6},{10,8},{12,10},{14,12},{0,14},{3,1},{5,3},... | collective-permute-start | bytes 589832 | tf_op jit(solution)/shard_map/ppermute | solution.py:234
  104.9 3.8 %collective-permute-start.27 = (bf16[32,3072]{1,0:T(8,128)(2,1)S(1)}, bf16[32,3072]{1,0:T(8,128)(2,1)S(1)}, u32[]{:S(2)}, u32[]{:S(2)}) collective-permute-start(bf16[32,3072]{1,0:T(8,128)(2,1)S(1)} %add_convert_fusion.1), channel_id=1, source_target_pairs={{2,0},{4,2},{6,4},{8,6},{10,8},{12,10},{14,12},{0,14},{3,1},{5,3},... | collective-permute-start | bytes 589832 | tf_op jit(solution)/shard_map/ppermute | solution.py:234
  109.5 3.8 %collective-permute-start.21 = (bf16[32,3072]{1,0:T(8,128)(2,1)S(1)}, bf16[32,3072]{1,0:T(8,128)(2,1)S(1)}, u32[]{:S(2)}, u32[]{:S(2)}) collective-permute-start(bf16[32,3072]{1,0:T(8,128)(2,1)S(1)} %add_convert_fusion.5), channel_id=1, source_target_pairs={{2,0},{4,2},{6,4},{8,6},{10,8},{12,10},{14,12},{0,14},{3,1},{5,3},... | collective-permute-start | bytes 589832 | tf_op jit(solution)/shard_map/ppermute | solution.py:234
  113.5 3.3 %collective-permute-start.28 = (bf16[32,3072]{1,0:T(8,128)(2,1)S(1)}, bf16[32,3072]{1,0:T(8,128)(2,1)S(1)}, u32[]{:S(2)}, u32[]{:S(2)}) collective-permute-start(bf16[32,3072]{1,0:T(8,128)(2,1)S(1)} %add_convert_fusion), channel_id=1, source_target_pairs={{2,0},{4,2},{6,4},{8,6},{10,8},{12,10},{14,12},{0,14},{3,1},{5,3},... | collective-permute-start | bytes 589832 | tf_op jit(solution)/shard_map/ppermute | solution.py:234
  116.8 3.5 %collective-permute-done.17 = bf16[32,3072]{1,0:T(8,128)(2,1)S(1)} collective-permute-done((bf16[32,3072]{1,0:T(8,128)(2,1)S(1)}, bf16[32,3072]{1,0:T(8,128)(2,1)S(1)}, u32[]{:S(2)}, u32[]{:S(2)}) %collective-permute-start.17) | collective-permute-done | bytes 196640 | tf_op jit(solution)/shard_map/ppermute | solution.py:231
  120.6 6.8 %collective-permute-done.18 = bf16[32,3072]{1,0:T(8,128)(2,1)S(1)} collective-permute-done((bf16[32,3072]{1,0:T(8,128)(2,1)S(1)}, bf16[32,3072]{1,0:T(8,128)(2,1)S(1)}, u32[]{:S(2)}, u32[]{:S(2)}) %collective-permute-start.18) | collective-permute-done | bytes 196640 | tf_op jit(solution)/shard_map/ppermute | solution.py:231
  (107 shorter events, 28.0 us)
Async XLA Ops:
  0.6 14.1 %collective-permute-start = (f32[64,3072]{1,0:T(8,128)}, f32[64,3072]{1,0:T(8,128)S(1)}, u32[]{:S(2)}, u32[]{:S(2)}) collective-permute-start(f32[64,3072]{1,0:T(8,128)} %bitcast.33), channel_id=1, source_target_pairs={{240,0},{0,16},{16,32},{32,48},{48,64},{64,80},{80,96},{96,112},{1... | collective-permute-start | bytes 2359304 | tf_op jit(solution)/shard_map/ppermute | solution.py:236
  17.8 11.9 %collective-permute-start.1 = (bf16[32,3072]{1,0:T(8,128)(2,1)}, bf16[32,3072]{1,0:T(8,128)(2,1)S(1)}, u32[]{:S(2)}, u32[]{:S(2)}) collective-permute-start(bf16[32,3072]{1,0:T(8,128)(2,1)} %get-tuple-element.45.refs_0_), channel_id=1, source_target_pairs={{0,2},{2,4},{4,6},{6,8},{8,10},{10,12},{12,14},{14,0},{1,3},{3,5},... | collective-permute-start | bytes 589832 | tf_op jit(solution)/shard_map/ppermute | solution.py:231
  19.7 14.2 %collective-permute-start.2 = (bf16[32,3072]{1,0:T(8,128)(2,1)}, bf16[32,3072]{1,0:T(8,128)(2,1)S(1)}, u32[]{:S(2)}, u32[]{:S(2)}) collective-permute-start(bf16[32,3072]{1,0:T(8,128)(2,1)} %get-tuple-element.46.refs_1_), channel_id=1, source_target_pairs={{0,2},{2,4},{4,6},{6,8},{8,10},{10,12},{12,14},{14,0},{1,3},{3,5},... | collective-permute-start | bytes 589832 | tf_op jit(solution)/shard_map/ppermute | solution.py:231
  21.7 12.3 %collective-permute-start.3 = (bf16[32,3072]{1,0:T(8,128)(2,1)}, bf16[32,3072]{1,0:T(8,128)(2,1)S(1)}, u32[]{:S(2)}, u32[]{:S(2)}) collective-permute-start(bf16[32,3072]{1,0:T(8,128)(2,1)} %get-tuple-element.45.refs_0_), channel_id=1, source_target_pairs={{2,0},{4,2},{6,4},{8,6},{10,8},{12,10},{14,12},{0,14},{3,1},{5,3},... | collective-permute-start | bytes 589832 | tf_op jit(solution)/shard_map/ppermute | solution.py:234
  23.8 13.4 %collective-permute-start.4 = (bf16[32,3072]{1,0:T(8,128)(2,1)}, bf16[32,3072]{1,0:T(8,128)(2,1)S(1)}, u32[]{:S(2)}, u32[]{:S(2)}) collective-permute-start(bf16[32,3072]{1,0:T(8,128)(2,1)} %get-tuple-element.46.refs_1_), channel_id=1, source_target_pairs={{2,0},{4,2},{6,4},{8,6},{10,8},{12,10},{14,12},{0,14},{3,1},{5,3},... | collective-permute-start | bytes 589832 | tf_op jit(solution)/shard_map/ppermute | solution.py:234
  29.7 23.3 %collective-permute-start.5 = (bf16[32,3072]{1,0:T(8,128)(2,1)S(1)}, bf16[32,3072]{1,0:T(8,128)(2,1)S(1)}, u32[]{:S(2)}, u32[]{:S(2)}) collective-permute-start(bf16[32,3072]{1,0:T(8,128)(2,1)S(1)} %collective-permute-done.1.refs_0_), channel_id=1, source_target_pairs={{0,2},{2,4},{4,6},{6,8},{8,10},{10,12},{12,14},{14,0},{1,3},{3,5},... | collective-permute-start | bytes 589832 | tf_op jit(solution)/shard_map/ppermute | solution.py:231
  33.9 20.4 %collective-permute-start.6 = (bf16[32,3072]{1,0:T(8,128)(2,1)S(1)}, bf16[32,3072]{1,0:T(8,128)(2,1)S(1)}, u32[]{:S(2)}, u32[]{:S(2)}) collective-permute-start(bf16[32,3072]{1,0:T(8,128)(2,1)S(1)} %collective-permute-done.2.refs_1_), channel_id=1, source_target_pairs={{0,2},{2,4},{4,6},{6,8},{8,10},{10,12},{12,14},{14,0},{1,3},{3,5},... | collective-permute-start | bytes 589832 | tf_op jit(solution)/shard_map/ppermute | solution.py:231
  33.9 20.5 %collective-permute-start.7 = (bf16[32,3072]{1,0:T(8,128)(2,1)S(1)}, bf16[32,3072]{1,0:T(8,128)(2,1)S(1)}, u32[]{:S(2)}, u32[]{:S(2)}) collective-permute-start(bf16[32,3072]{1,0:T(8,128)(2,1)S(1)} %collective-permute-done.3.refs_2_), channel_id=1, source_target_pairs={{2,0},{4,2},{6,4},{8,6},{10,8},{12,10},{14,12},{0,14},{3,1},{5,3},... | collective-permute-start | bytes 589832 | tf_op jit(solution)/shard_map/ppermute | solution.py:234
  37.2 20.4 %collective-permute-start.8 = (bf16[32,3072]{1,0:T(8,128)(2,1)S(1)}, bf16[32,3072]{1,0:T(8,128)(2,1)S(1)}, u32[]{:S(2)}, u32[]{:S(2)}) collective-permute-start(bf16[32,3072]{1,0:T(8,128)(2,1)S(1)} %collective-permute-done.4.refs_3_), channel_id=1, source_target_pairs={{2,0},{4,2},{6,4},{8,6},{10,8},{12,10},{14,12},{0,14},{3,1},{5,3},... | collective-permute-start | bytes 589832 | tf_op jit(solution)/shard_map/ppermute | solution.py:234
  53.0 14.5 %collective-permute-start.9 = (bf16[32,3072]{1,0:T(8,128)(2,1)S(1)}, bf16[32,3072]{1,0:T(8,128)(2,1)S(1)}, u32[]{:S(2)}, u32[]{:S(2)}) collective-permute-start(bf16[32,3072]{1,0:T(8,128)(2,1)S(1)} %collective-permute-done.5.refs_0_), channel_id=1, source_target_pairs={{0,2},{2,4},{4,6},{6,8},{8,10},{10,12},{12,14},{14,0},{1,3},{3,5},... | collective-permute-start | bytes 589832 | tf_op jit(solution)/shard_map/ppermute | solution.py:231
  54.3 13.2 %collective-permute-start.10 = (bf16[32,3072]{1,0:T(8,128)(2,1)S(1)}, bf16[32,3072]{1,0:T(8,128)(2,1)S(1)}, u32[]{:S(2)}, u32[]{:S(2)}) collective-permute-start(bf16[32,3072]{1,0:T(8,128)(2,1)S(1)} %collective-permute-done.6.refs_1_), channel_id=1, source_target_pairs={{0,2},{2,4},{4,6},{6,8},{8,10},{10,12},{12,14},{14,0},{1,3},{3,5},... | collective-permute-start | bytes 589832 | tf_op jit(solution)/shard_map/ppermute | solution.py:231
  54.4 13.1 %collective-permute-start.11 = (bf16[32,3072]{1,0:T(8,128)(2,1)S(1)}, bf16[32,3072]{1,0:T(8,128)(2,1)S(1)}, u32[]{:S(2)}, u32[]{:S(2)}) collective-permute-start(bf16[32,3072]{1,0:T(8,128)(2,1)S(1)} %collective-permute-done.7.refs_2_), channel_id=1, source_target_pairs={{2,0},{4,2},{6,4},{8,6},{10,8},{12,10},{14,12},{0,14},{3,1},{5,3},... | collective-permute-start | bytes 589832 | tf_op jit(solution)/shard_map/ppermute | solution.py:234
  57.6 10.0 %collective-permute-start.12 = (bf16[32,3072]{1,0:T(8,128)(2,1)S(1)}, bf16[32,3072]{1,0:T(8,128)(2,1)S(1)}, u32[]{:S(2)}, u32[]{:S(2)}) collective-permute-start(bf16[32,3072]{1,0:T(8,128)(2,1)S(1)} %collective-permute-done.8.refs_3_), channel_id=1, source_target_pairs={{2,0},{4,2},{6,4},{8,6},{10,8},{12,10},{14,12},{0,14},{3,1},{5,3},... | collective-permute-start | bytes 589832 | tf_op jit(solution)/shard_map/ppermute | solution.py:234
  85.1 12.1 %collective-permute-start.25 = (bf16[32,3072]{1,0:T(8,128)(2,1)S(1)}, bf16[32,3072]{1,0:T(8,128)(2,1)S(1)}, u32[]{:S(2)}, u32[]{:S(2)}) collective-permute-start(bf16[32,3072]{1,0:T(8,128)(2,1)S(1)} %get-tuple-element.84), channel_id=1, source_target_pairs={{2,0},{4,2},{6,4},{8,6},{10,8},{12,10},{14,12},{0,14},{3,1},{5,3},... | collective-permute-start | bytes 589832 | tf_op jit(solution)/shard_map/ppermute | solution.py:234
  89.6 11.0 %collective-permute-start.22 = (bf16[32,3072]{1,0:T(8,128)(2,1)S(1)}, bf16[32,3072]{1,0:T(8,128)(2,1)S(1)}, u32[]{:S(2)}, u32[]{:S(2)}) collective-permute-start(bf16[32,3072]{1,0:T(8,128)(2,1)S(1)} %get-tuple-element.81), channel_id=1, source_target_pairs={{0,2},{2,4},{4,6},{6,8},{8,10},{10,12},{12,14},{14,0},{1,3},{3,5},... | collective-permute-start | bytes 589832 | tf_op jit(solution)/shard_map/ppermute | solution.py:231
  89.7 11.1 %collective-permute-start.19 = (bf16[32,3072]{1,0:T(8,128)(2,1)S(1)}, bf16[32,3072]{1,0:T(8,128)(2,1)S(1)}, u32[]{:S(2)}, u32[]{:S(2)}) collective-permute-start(bf16[32,3072]{1,0:T(8,128)(2,1)S(1)} %get-tuple-element.77), channel_id=1, source_target_pairs={{2,0},{4,2},{6,4},{8,6},{10,8},{12,10},{14,12},{0,14},{3,1},{5,3},... | collective-permute-start | bytes 589832 | tf_op jit(solution)/shard_map/ppermute | solution.py:234
  92.9 11.2 %collective-permute-start.15 = (bf16[32,3072]{1,0:T(8,128)(2,1)S(1)}, bf16[32,3072]{1,0:T(8,128)(2,1)S(1)}, u32[]{:S(2)}, u32[]{:S(2)}) collective-permute-start(bf16[32,3072]{1,0:T(8,128)(2,1)S(1)} %get-tuple-element.61), channel_id=1, source_target_pairs={{0,2},{2,4},{4,6},{6,8},{8,10},{10,12},{12,14},{14,0},{1,3},{3,5},... | collective-permute-start | bytes 589832 | tf_op jit(solution)/shard_map/ppermute | solution.py:231
  97.3 7.5 %collective-permute-start.26 = (bf16[32,3072]{1,0:T(8,128)(2,1)S(1)}, bf16[32,3072]{1,0:T(8,128)(2,1)S(1)}, u32[]{:S(2)}, u32[]{:S(2)}) collective-permute-start(bf16[32,3072]{1,0:T(8,128)(2,1)S(1)} %add_convert_fusion.2), channel_id=1, source_target_pairs={{2,0},{4,2},{6,4},{8,6},{10,8},{12,10},{14,12},{0,14},{3,1},{5,3},... | collective-permute-start | bytes 589832 | tf_op jit(solution)/shard_map/ppermute | solution.py:234
  100.7 8.0 %collective-permute-start.23 = (bf16[32,3072]{1,0:T(8,128)(2,1)S(1)}, bf16[32,3072]{1,0:T(8,128)(2,1)S(1)}, u32[]{:S(2)}, u32[]{:S(2)}) collective-permute-start(bf16[32,3072]{1,0:T(8,128)(2,1)S(1)} %add_convert_fusion.4), channel_id=1, source_target_pairs={{0,2},{2,4},{4,6},{6,8},{8,10},{10,12},{12,14},{14,0},{1,3},{3,5},... | collective-permute-start | bytes 589832 | tf_op jit(solution)/shard_map/ppermute | solution.py:231
  100.8 8.6 %collective-permute-start.20 = (bf16[32,3072]{1,0:T(8,128)(2,1)S(1)}, bf16[32,3072]{1,0:T(8,128)(2,1)S(1)}, u32[]{:S(2)}, u32[]{:S(2)}) collective-permute-start(bf16[32,3072]{1,0:T(8,128)(2,1)S(1)} %add_convert_fusion.6), channel_id=1, source_target_pairs={{2,0},{4,2},{6,4},{8,6},{10,8},{12,10},{14,12},{0,14},{3,1},{5,3},... | collective-permute-start | bytes 589832 | tf_op jit(solution)/shard_map/ppermute | solution.py:234
  104.2 9.1 %collective-permute-start.16 = (bf16[32,3072]{1,0:T(8,128)(2,1)S(1)}, bf16[32,3072]{1,0:T(8,128)(2,1)S(1)}, u32[]{:S(2)}, u32[]{:S(2)}) collective-permute-start(bf16[32,3072]{1,0:T(8,128)(2,1)S(1)} %add_convert_fusion.9), channel_id=1, source_target_pairs={{0,2},{2,4},{4,6},{6,8},{8,10},{10,12},{12,14},{14,0},{1,3},{3,5},... | collective-permute-start | bytes 589832 | tf_op jit(solution)/shard_map/ppermute | solution.py:231
  104.9 8.6 %collective-permute-start.27 = (bf16[32,3072]{1,0:T(8,128)(2,1)S(1)}, bf16[32,3072]{1,0:T(8,128)(2,1)S(1)}, u32[]{:S(2)}, u32[]{:S(2)}) collective-permute-start(bf16[32,3072]{1,0:T(8,128)(2,1)S(1)} %add_convert_fusion.1), channel_id=1, source_target_pairs={{2,0},{4,2},{6,4},{8,6},{10,8},{12,10},{14,12},{0,14},{3,1},{5,3},... | collective-permute-start | bytes 589832 | tf_op jit(solution)/shard_map/ppermute | solution.py:234
  108.7 11.8 %collective-permute-start.24 = (bf16[32,3072]{1,0:T(8,128)(2,1)S(1)}, bf16[32,3072]{1,0:T(8,128)(2,1)S(1)}, u32[]{:S(2)}, u32[]{:S(2)}) collective-permute-start(bf16[32,3072]{1,0:T(8,128)(2,1)S(1)} %add_convert_fusion.3), channel_id=1, source_target_pairs={{0,2},{2,4},{4,6},{6,8},{8,10},{10,12},{12,14},{14,0},{1,3},{3,5},... | collective-permute-start | bytes 589832 | tf_op jit(solution)/shard_map/ppermute | solution.py:231
  109.5 11.0 %collective-permute-start.21 = (bf16[32,3072]{1,0:T(8,128)(2,1)S(1)}, bf16[32,3072]{1,0:T(8,128)(2,1)S(1)}, u32[]{:S(2)}, u32[]{:S(2)}) collective-permute-start(bf16[32,3072]{1,0:T(8,128)(2,1)S(1)} %add_convert_fusion.5), channel_id=1, source_target_pairs={{2,0},{4,2},{6,4},{8,6},{10,8},{12,10},{14,12},{0,14},{3,1},{5,3},... | collective-permute-start | bytes 589832 | tf_op jit(solution)/shard_map/ppermute | solution.py:234
  (20 other events, 129.8 us)
